TPU v7x, 32 devices: a whole 2x2x4 slice. The times are simulated.
32 devices in a mesh: rows: 16 (over z, y, x), cols: 2 (over core).
Axes of the slice: x: 2, y: 2, z: 4, core: 2. Of those that a mesh axis runs over, the one named last changes fastest.
Arguments:
- node_feat: bfloat16 [16, 2, 128, 256], P('rows', 'cols'), may hold values from -6 to 6
- species: int32 [16, 2, 128], P('rows', 'cols'), may hold values from 0 to 1
- layer_embed: bfloat16 [2, 256], replicated, may hold values from -6 to 6
- w_src: bfloat16 [256, 128], replicated, may hold values from -0.375 to 0.375
- w_dst: bfloat16 [256, 128], replicated, may hold values from -0.375 to 0.375
- w_rad: float32 [16, 128], replicated, may hold values from -3 to 3
- w_mid: bfloat16 [128, 128], replicated, may hold values from -0.5 to 0.5
- w_out: bfloat16 [128, 169], replicated, may hold values from -0.5 to 0.5
- w_self: bfloat16 [256, 169], replicated, may hold values from -0.375 to 0.375
- bond_target: int32 [16, 2, 24, 128], P('rows', 'cols'), may hold values from 0 to 1151, as said below
- bond_live: int32 [16, 2, 24, 128], P('rows', 'cols'), may hold values from 0 to 1
- bond_len: float32 [16, 2, 24, 128], P('rows', 'cols'), may hold values from 1.4 to 6
- probes: float32 [16, 2, 128, 208], P('rows', 'cols'), may hold values from -6 to 6
- cheb_coef: float32 [5], replicated, may hold values from -1 to 1
Outputs:
- fermi_probes: float32 [16, 2, 128, 208], P('rows', 'cols')
Inputs may be any that keep to these rules, and one draw needn't show every extreme that they name: bond_target = b * 128 + j names atom j of the block at offset (b // 3 - 1, b % 3 - 1) in (long, short) direction from the bond's own block.
All inputs are finite; a program needn't handle non-finite values.
Results may differ from a plain program's by a relative error of at most 0.008.
Values may be sent and summed in bfloat16 or wider, within the bound.
A program may use at most 128 MiB of HBM per device.

v0:
```python
import functools

import jax
import jax.numpy as jnp
from jax import lax
from jax.experimental import pallas as pl
from jax.experimental.pallas import tpu as pltpu
from jax.sharding import PartitionSpec as P

RADIAL = 16
ORBITALS = 13
PROBES = 16
STEPS = 4
VEC = ORBITALS * PROBES
PAIRS = ORBITALS * ORBITALS
SPAN = 176

stretch_factor = 6.0
basis_sharpness = 1.5
MESH = pl.DeviceIdType.MESH
f32 = jnp.float32
bf16 = jnp.bfloat16


def silu(x):
    return x * (0.5 * jnp.tanh(0.5 * x) + 0.5)


def dot_tn(a, b):
    return lax.dot_general(a, b, (((0,), (0,)), ((), ())), preferred_element_type=f32)


def kernel(
    n_rows,
    rounds,
    node_ref,
    species_ref,
    embed_ref,
    wsrc_ref,
    wdst_ref,
    wrad_ref,
    wmid_ref,
    wout_ref,
    wself_ref,
    tgt_ref,
    live_ref,
    len_ref,
    probes_ref,
    coef_ref,
    out_ref,
    first,
    vecs,
    onehot,
    index,
    blocks,
    source,
    split,
    keep,
    wide,
    tall,
    rad,
    far,
    send_sem,
    recv_sem,
    rsend_sem,
    rrecv_sem,
):
    atoms = node_ref.shape[0]
    slots = tgt_ref.shape[0]
    channels = wsrc_ref.shape[1]
    r = lax.axis_index("rows")
    c = lax.axis_index("cols")
    oc = 1 - c
    has_up = r > 0
    has_down = r < n_rows - 1
    ways = [
        (-1, 0, has_up),
        (-1, 1, has_up),
        (1, 0, has_down),
        (1, 1, has_down),
        (0, 1, None),
    ]

    def when(cond, fn):
        if cond is None:
            fn()
        else:
            pl.when(cond)(fn)

    def place(step, other):
        return (step + 1) * 2 + other

    def partner(q):
        if q == 0:
            return (r, oc)
        w = 1 << (q - 1)
        return (r + w - 2 * w * ((r // w) % 2), c)

    barrier = pltpu.get_barrier_semaphore()
    for step, other, cond in ways:

        def greet(step=step, other=other):
            pl.semaphore_signal(
                barrier, inc=1, device_id=(r + step, oc if other else c), device_id_type=MESH
            )

        when(cond, greet)
    for q in range(1, rounds):
        pl.semaphore_signal(barrier, inc=1, device_id=partner(q), device_id_type=MESH)

    species_col = jnp.broadcast_to(species_ref[...].astype(f32), (atoms, atoms)).T
    species_col = jnp.concatenate([species_col] * (node_ref.shape[1] // atoms), axis=1)
    embed = embed_ref[...].astype(f32)
    mixed = (
        node_ref[...].astype(f32)
        + jnp.where(species_col == 0.0, embed[0:1, :], embed[1:2, :])
    ).astype(bf16)
    target = jnp.dot(mixed, wdst_ref[...], preferred_element_type=f32)
    own = pl.ds(place(0, 0) * atoms, atoms)
    first[0:channels, own] = target.T.astype(bf16)
    wide[...] = jnp.zeros_like(wide)
    wide[:, 0:VEC] = probes_ref[...]
    start = jnp.concatenate(
        [wide[:, i * atoms : (i + 1) * atoms].T for i in range(wide.shape[1] // atoms)], axis=0
    )[0:VEC]
    keep[0] = start
    first[channels : channels + VEC, own] = start.astype(bf16)

    for cond, step in ((has_up, -1), (has_down, 1)):

        def clear(step=step):
            cols = pl.ds(place(step, 0) * atoms, 2 * atoms)
            first[:, cols] = jnp.zeros((first.shape[0], 2 * atoms), bf16)
            for n in range(STEPS - 1):
                vecs[n, :, cols] = jnp.zeros((VEC, 2 * atoms), bf16)

        pl.when(jnp.logical_not(cond))(clear)

    def buffer(n):
        return first if n == 0 else vecs.at[n - 1]

    def copy(n, w, arriving):
        buf = buffer(n)
        step, other, _ = ways[w]
        back = w if step == 0 else (w + 2) % 4
        to = place(step, other) if arriving else place(-step, other)
        return pltpu.make_async_remote_copy(
            src_ref=buf.at[:, own],
            dst_ref=buf.at[:, pl.ds(to * atoms, atoms)],
            send_sem=send_sem.at[n, w],
            recv_sem=recv_sem.at[n, w if arriving else back],
            device_id=(r + step, oc if other else c),
            device_id_type=MESH,
        )

    def send(n):
        for w, (_, _, cond) in enumerate(ways):
            when(cond, lambda w=w: copy(n, w, False).start())

    def receive(n):
        for w, (_, _, cond) in enumerate(ways):
            when(cond, lambda w=w: copy(n, w, True).wait_recv())

    def finish(n):
        for w, (_, _, cond) in enumerate(ways):
            when(cond, lambda w=w: copy(n, w, False).wait_send())

    pl.semaphore_wait(
        barrier, rounds + 2 * jnp.where(has_up, 1, 0) + 2 * jnp.where(has_down, 1, 0)
    )
    send(0)

    bt = tgt_ref[...]
    b = bt // atoms
    dr = jnp.where(b >= 3, 1, 0) + jnp.where(b >= 6, 1, 0)
    dc = b - 3 * dr - 1
    other = jnp.where(dc == oc - c, 1, 0)
    valid = (dc == 0) | (dc == oc - c)
    index[...] = jnp.where(valid, (dr * 2 + other) * atoms + (bt - b * atoms), -1)
    two = 2 * atoms

    def pair_row(ref, k):
        return jnp.concatenate([ref[pl.ds(2 * k, 1), :], ref[pl.ds(2 * k + 1, 1), :]], axis=1)

    def mark(k, carry):
        row = pair_row(index, k)
        ids = lax.broadcasted_iota(jnp.int32, (6 * atoms, two), 0)
        onehot[k] = jnp.where(ids == row, 1.0, 0.0).astype(bf16)
        return carry

    lax.fori_loop(0, slots // 2, mark, 0)

    source_t = jnp.dot(mixed, wsrc_ref[...], preferred_element_type=f32).T
    source_t = source_t.astype(bf16).astype(f32)
    source[...] = jnp.concatenate([source_t, source_t], axis=1)
    wrad = wrad_ref[...]
    w_hi = wrad.astype(bf16)
    w_lo = (wrad - w_hi.astype(f32)).astype(bf16)
    split[...] = jnp.concatenate([w_hi, w_hi, w_lo], axis=0)
    centers = 1.0 + 5.0 * lax.broadcasted_iota(jnp.int32, (RADIAL, two), 0).astype(f32) / (
        RADIAL - 1
    )
    raw = lax.dot_general(
        wself_ref[...], mixed, (((0,), (1,)), ((), ())), preferred_element_type=f32
    )
    far[0:PAIRS, 0:atoms] = raw
    for i in range(ORBITALS):
        for j in range(i, ORBITALS):
            p, q = i * ORBITALS + j, j * ORBITALS + i
            mean = 0.5 * (far[p : p + 1, 0:atoms] + far[q : q + 1, 0:atoms])
            mean = mean.astype(bf16).astype(f32)
            blocks[slots, p : p + 1, :] = mean
            if p != q:
                blocks[slots, q : q + 1, :] = mean

    def block_apply(k, parts, acc):
        acc = list(acc)
        for j in range(ORBITALS):
            n = parts(j)
            for i in range(ORBITALS):
                acc[i] = acc[i] + blocks[k, pl.ds(i * ORBITALS + j, 1), :] * n
        return tuple(acc)

    def own_apply(vec, acc):
        return block_apply(slots, lambda j: vec[j * PROBES : (j + 1) * PROBES], acc)

    def gathered(k, acc):
        for h in range(2):
            acc = block_apply(
                2 * k + h,
                lambda j: far[
                    channels + j * PROBES : channels + (j + 1) * PROBES,
                    h * atoms : (h + 1) * atoms,
                ],
                acc,
            )
        return acc

    zero = tuple(jnp.zeros((PROBES, atoms), f32) for _ in range(ORBITALS))
    receive(0)

    def bond_step(k, carry):
        acc, total = carry
        far[...] = jnp.dot(first[...], onehot[k], preferred_element_type=f32)
        length = pair_row(len_ref, k)
        basis = jnp.exp(-basis_sharpness * (length - centers) ** 2)
        b_hi = basis.astype(bf16)
        b_lo = (basis - b_hi.astype(f32)).astype(bf16)
        lifted = dot_tn(split[...], jnp.concatenate([b_hi, b_lo, b_hi], axis=0))
        edge = silu(source[...] + far[0:channels, :] + lifted).astype(bf16)
        hidden = silu(dot_tn(wmid_ref[...], edge)).astype(bf16)
        made = dot_tn(wout_ref[...], hidden) * pair_row(live_ref, k).astype(f32)
        made = made.astype(bf16).astype(f32)
        blocks[2 * k, 0:PAIRS, :] = made[:, 0:atoms]
        blocks[2 * k + 1, 0:PAIRS, :] = made[:, atoms:two]
        tall[0:PAIRS, :] += jnp.abs(made[:, 0:atoms]) + jnp.abs(made[:, atoms:two])
        return gathered(k, acc), total

    tall[0:PAIRS, :] = jnp.abs(blocks[slots, 0:PAIRS, :])
    acc, _ = lax.fori_loop(0, slots // 2, bond_step, (own_apply(keep[0], zero), 0))
    y1 = jnp.concatenate(acc, axis=0)
    vecs[0, :, own] = y1.astype(bf16)
    send(1)
    keep[1] = y1

    biggest = jnp.zeros((1, atoms), f32)
    for i in range(ORBITALS):
        row = jnp.sum(tall[i * ORBITALS : (i + 1) * ORBITALS, :], axis=0, keepdims=True)
        biggest = jnp.maximum(biggest, row)
    rad[0] = jnp.broadcast_to(biggest, rad.shape[1:])

    def radius_copy(q):
        return pltpu.make_async_remote_copy(
            src_ref=rad.at[q],
            dst_ref=rad.at[rounds + 1 + q],
            send_sem=rsend_sem.at[q],
            recv_sem=rrecv_sem.at[q],
            device_id=partner(q),
            device_id_type=MESH,
        )

    def radius_turn(q):
        radius_copy(q).wait_recv()
        rad[q + 1] = jnp.maximum(rad[q], rad[rounds + 1 + q])
        if q + 1 < rounds:
            radius_copy(q + 1).start()

    radius_copy(0).start()

    def apply_part(n, lo, hi, acc):
        def step(k, acc):
            far[pl.ds(channels, VEC), :] = jnp.dot(
                vecs[n - 1], onehot[k], preferred_element_type=f32
            )
            return gathered(k, acc)

        return lax.fori_loop(lo, hi, step, acc)

    half = slots // 2
    acc = own_apply(y1, zero)
    radius_turn(0)
    radius_turn(1)
    receive(1)
    turns = list(range(2, rounds))
    cuts = [half * i // (len(turns) + 1) for i in range(len(turns) + 2)]
    for i in range(len(turns) + 1):
        acc = apply_part(1, cuts[i], cuts[i + 1], acc)
        if i < len(turns):
            radius_turn(turns[i])
    radius = jnp.max(rad[rounds], keepdims=True)
    scale = stretch_factor / radius

    t0 = keep[0]
    t1 = scale[0:1, 0:1] * keep[1]
    t2 = 2.0 * (scale[0:1, 0:1] * (scale[0:1, 0:1] * jnp.concatenate(acc, axis=0))) - t0
    vecs[1, :, own] = t2.astype(bf16)
    send(2)
    keep[1] = t1
    keep[2] = t2
    keep[0] = coef_ref[0] * t0 + coef_ref[1] * t1 + coef_ref[2] * t2
    acc = own_apply(keep[2], zero)
    receive(2)
    acc = apply_part(2, 0, half, acc)
    t3 = 2.0 * (scale[0:1, 0:1] * jnp.concatenate(acc, axis=0)) - keep[1]
    vecs[2, :, own] = t3.astype(bf16)
    send(3)
    keep[1] = t3
    keep[0] = keep[0] + coef_ref[3] * t3
    acc = own_apply(keep[1], zero)
    receive(3)
    acc = apply_part(3, 0, half, acc)
    t4 = 2.0 * (scale[0:1, 0:1] * jnp.concatenate(acc, axis=0)) - keep[2]
    tall[0:VEC, :] = keep[0] + coef_ref[4] * t4
    tall[VEC:, :] = jnp.zeros((tall.shape[0] - VEC, atoms), f32)
    for i in range(tall.shape[0] // atoms):
        wide[:, i * atoms : (i + 1) * atoms] = tall[i * atoms : (i + 1) * atoms, :].T
    out_ref[...] = wide[:, 0:VEC]
    for n in range(STEPS):
        finish(n)
    for q in range(rounds):
        radius_copy(q).wait_send()


def body(n_rows, *args):
    (node, species, embed, wsrc, wdst, wrad, wmid, wout, wself, tgt, live, length, probes, coef) = args
    atoms = node.shape[2]
    slots = tgt.shape[2]
    channels = wsrc.shape[1]
    rounds = n_rows.bit_length()
    vmem = pl.BlockSpec(memory_space=pltpu.VMEM)
    lanes = 2 * atoms
    tall_rows = 2 * atoms
    out = pl.pallas_call(
        functools.partial(kernel, n_rows, rounds),
        out_shape=jax.ShapeDtypeStruct((atoms, VEC), f32),
        in_specs=[vmem] * 13 + [pl.BlockSpec(memory_space=pltpu.SMEM)],
        out_specs=vmem,
        scratch_shapes=[
            pltpu.VMEM((channels + VEC, 6 * atoms), bf16),
            pltpu.VMEM((STEPS - 1, VEC, 6 * atoms), bf16),
            pltpu.VMEM((slots // 2, 6 * atoms, lanes), bf16),
            pltpu.VMEM((slots, atoms), jnp.int32),
            pltpu.VMEM((slots + 1, SPAN, atoms), f32),
            pltpu.VMEM((channels, lanes), f32),
            pltpu.VMEM((3 * RADIAL, channels), bf16),
            pltpu.VMEM((3, VEC, atoms), f32),
            pltpu.VMEM((atoms, tall_rows), f32),
            pltpu.VMEM((tall_rows, atoms), f32),
            pltpu.VMEM((2 * rounds + 1, 8, atoms), f32),
            pltpu.VMEM((channels + VEC, lanes), f32),
            pltpu.SemaphoreType.DMA((STEPS, 5)),
            pltpu.SemaphoreType.DMA((STEPS, 5)),
            pltpu.SemaphoreType.DMA((rounds,)),
            pltpu.SemaphoreType.DMA((rounds,)),
        ],
        compiler_params=pltpu.CompilerParams(
            collective_id=0, has_side_effects=True, vmem_limit_bytes=40 * 1024 * 1024
        ),
    )(
        node[0, 0], species[0], embed, wsrc, wdst, wrad, wmid, wout, wself,
        tgt[0, 0], live[0, 0], length[0, 0], probes[0, 0], coef,
    )
    return out[None, None]


def solution(mesh):
    n_rows = mesh.shape["rows"]
    block4 = P("rows", "cols", None, None)
    placed = (
        block4, P("rows", "cols", None), P(), P(), P(), P(), P(), P(), P(),
        block4, block4, block4, block4, P(),
    )
    return jax.shard_map(
        functools.partial(body, n_rows), mesh=mesh, in_specs=placed, out_specs=block4, check_vma=False
    )
```

profile of v0, /device:TPU:7, one launch (start us, length us, event | category | flops | bytes accessed | tf_op | source)
XLA Modules:
  0.0 68.6 jit_solution(9365825724778657077)
XLA Ops:
  0.0 0.0 copy-start.12
  0.0 0.9 %copy.16.wout_ref = bf16[128,169]{1,0:T(8,128)(2,1)S(1)} copy(bf16[128,169]{0,1:T(8,128)(2,1)} %param.21) | data formatting | bytes 86528 | tf_op args[7]
  0.9 0.0 copy-done.12
  0.9 0.0 copy-start.11
  1.0 0.0 copy-start.4
  1.0 0.0 copy-start.5
  1.0 0.0 copy-start.6
  1.0 0.0 copy-start.10
  1.0 0.1 copy.17.wself_ref
  1.1 0.7 %copy-done.11 = f32[1,1,128,208]{2,3,1,0:T(8,128)S(1)} copy-done((f32[1,1,128,208]{2,3,1,0:T(8,128)S(1)}, f32[1,1,128,208]{2,3,1,0:T(8,128)}, u32[]{:S(2)}) %copy-start.11) | copy-done | bytes 106520
  1.8 0.0 copy-start
  1.8 0.0 copy-start.1
  1.8 0.0 copy-start.2
  1.8 0.0 copy-start.3
  1.8 0.0 copy-start.7
  1.9 0.1 copy.15
  2.0 0.0 copy-start.8
  2.0 0.0 copy-start.9
  2.0 0.0 copy-done.4
  2.0 0.0 copy-done.5
  2.0 0.0 copy-done.6
  2.0 0.0 copy-done.10
  2.0 0.6 copy-done
  2.7 0.0 copy-done.1
  2.7 0.0 copy-done.2
  2.7 0.0 copy-done.3
  2.7 0.0 copy-done.7
  2.7 0.0 copy-done.8
  2.7 0.0 copy-done.9
  2.8 65.1 %shard_map.136 = f32[128,208]{1,0:T(8,128)S(1)} custom-call(bf16[128,256]{1,0:T(8,128)(2,1)S(1)} %bitcast.9, s32[1,128]{1,0:T(1,128)S(1)} %bitcast.13, bf16[2,256]{1,0:T(2,128)(2,1)S(1)} %copy-done.8, bf16[256,128]{1,0:T(8,128)(2,1)S(1)} %copy-done.1, bf16[256,128]{1,0:T(8,128)(2,1)S(1)} %copy-done.2, f32[16,128]{1,0:T(8,128)S(1)} %copy-done.7, ...), custom_call_target="tpu_custom_call" | custom-call | tf_op jit(solution)/shard_map/pallas_call | solution.py:353
  67.8 0.7 %copy.18 = f32[1,1,128,208]{2,3,1,0:T(8,128)} copy(f32[1,1,128,208]{3,2,1,0:T(8,128)S(1)} %bitcast.7) | data formatting | bytes 212992 | tf_op jit(solution)/shard_map/broadcast_in_dim | solution.py:383
Async XLA Ops:
  0.0 0.9 %copy-start.12 = (bf16[256,169]{0,1:T(8,128)(2,1)S(1)}, bf16[256,169]{0,1:T(8,128)(2,1)}, u32[]{:S(2)}) copy-start(bf16[256,169]{0,1:T(8,128)(2,1)} %param.22) | copy-start | bytes 259588
  0.9 0.9 %copy-start.11 = (f32[1,1,128,208]{2,3,1,0:T(8,128)S(1)}, f32[1,1,128,208]{2,3,1,0:T(8,128)}, u32[]{:S(2)}) copy-start(f32[1,1,128,208]{2,3,1,0:T(8,128)} %param.26) | copy-start | bytes 319492
  1.0 1.0 %copy-start.4 = (s32[1,1,24,128]{3,2,1,0:T(8,128)S(1)}, s32[1,1,24,128]{3,2,1,0:T(8,128)}, u32[]{:S(2)}) copy-start(s32[1,1,24,128]{3,2,1,0:T(8,128)} %param.23) | copy-start | bytes 36868
  1.0 1.0 %copy-start.5 = (s32[1,1,24,128]{3,2,1,0:T(8,128)S(1)}, s32[1,1,24,128]{3,2,1,0:T(8,128)}, u32[]{:S(2)}) copy-start(s32[1,1,24,128]{3,2,1,0:T(8,128)} %param.24) | copy-start | bytes 36868
  1.0 1.0 %copy-start.6 = (f32[1,1,24,128]{3,2,1,0:T(8,128)S(1)}, f32[1,1,24,128]{3,2,1,0:T(8,128)}, u32[]{:S(2)}) copy-start(f32[1,1,24,128]{3,2,1,0:T(8,128)} %param.25) | copy-start | bytes 36868
  1.0 1.0 %copy-start.10 = (f32[5]{0:T(128)S(1)}, f32[5]{0:T(128)}, u32[]{:S(2)}) copy-start(f32[5]{0:T(128)} %coef_ref.1) | copy-start | bytes 64
  1.8 0.8 %copy-start = (bf16[1,1,128,256]{3,2,1,0:T(8,128)(2,1)S(1)}, bf16[1,1,128,256]{3,2,1,0:T(8,128)(2,1)}, u32[]{:S(2)}) copy-start(bf16[1,1,128,256]{3,2,1,0:T(8,128)(2,1)} %param.14) | copy-start | bytes 196612
  1.8 0.9 %copy-start.1 = (bf16[256,128]{1,0:T(8,128)(2,1)S(1)}, bf16[256,128]{1,0:T(8,128)(2,1)}, u32[]{:S(2)}) copy-start(bf16[256,128]{1,0:T(8,128)(2,1)} %wsrc_ref.1) | copy-start | bytes 196612
  1.8 0.9 %copy-start.2 = (bf16[256,128]{1,0:T(8,128)(2,1)S(1)}, bf16[256,128]{1,0:T(8,128)(2,1)}, u32[]{:S(2)}) copy-start(bf16[256,128]{1,0:T(8,128)(2,1)} %wdst_ref.1) | copy-start | bytes 196612
  1.8 0.9 %copy-start.3 = (bf16[128,128]{1,0:T(8,128)(2,1)S(1)}, bf16[128,128]{1,0:T(8,128)(2,1)}, u32[]{:S(2)}) copy-start(bf16[128,128]{1,0:T(8,128)(2,1)} %wmid_ref.1) | copy-start | bytes 98308
  1.8 0.9 %copy-start.7 = (f32[16,128]{1,0:T(8,128)S(1)}, f32[16,128]{1,0:T(8,128)}, u32[]{:S(2)}) copy-start(f32[16,128]{1,0:T(8,128)} %wrad_ref.1) | copy-start | bytes 24580
  2.0 0.8 %copy-start.8 = (bf16[2,256]{1,0:T(2,128)(2,1)S(1)}, bf16[2,256]{1,0:T(2,128)(2,1)}, u32[]{:S(2)}) copy-start(bf16[2,256]{1,0:T(2,128)(2,1)} %embed_ref.1) | copy-start | bytes 3076
  2.0 0.8 %copy-start.9 = (s32[1,1,128]{2,1,0:T(1,128)S(1)}, s32[1,1,128]{2,1,0:T(1,128)}, u32[]{:S(2)}) copy-start(s32[1,1,128]{2,1,0:T(1,128)} %param.15) | copy-start | bytes 1540
where the time goes:
time: 68.8 us; the launch traced here: 68.6 us
  Pallas kernels  65.1 us (95%)
  local copies, waits for them, and re-layouts  3.36 us (5%)
    pallas_call x1, Pallas kernels, body(): pl.pallas_call(functools.partial(kernel, n_rows, rounds), out_shape=jax.S...  65.1 us
    unnamed x29, local copies, waits for them, and re-layouts  2.62 us

commit v1 on v0

--- a/solution.py
+++ b/solution.py
@@ -60,6 +60,7 @@
     tall,
     rad,
     far,
+    near,
     send_sem,
     recv_sem,
     rsend_sem,
@@ -142,6 +143,15 @@
     def copy(n, w, arriving):
         buf = buffer(n)
         step, other, _ = ways[w]
+        if step != 0 and other:
+            return pltpu.make_async_remote_copy(
+                src_ref=buf.at[:, pl.ds(place(step, 0) * atoms, atoms)],
+                dst_ref=buf.at[:, pl.ds(place(step, 1) * atoms, atoms)],
+                send_sem=send_sem.at[n, w],
+                recv_sem=recv_sem.at[n, w],
+                device_id=(r, oc),
+                device_id_type=MESH,
+            )
         back = w if step == 0 else (w + 2) % 4
         to = place(step, other) if arriving else place(-step, other)
         return pltpu.make_async_remote_copy(
@@ -154,12 +164,19 @@
         )
 
     def send(n):
-        for w, (_, _, cond) in enumerate(ways):
-            when(cond, lambda w=w: copy(n, w, False).start())
+        for w in (0, 2, 4):
+            when(ways[w][2], lambda w=w: copy(n, w, False).start())
 
     def receive(n):
-        for w, (_, _, cond) in enumerate(ways):
-            when(cond, lambda w=w: copy(n, w, True).wait_recv())
+        for w in (0, 2):
+
+            def forward(w=w):
+                copy(n, w, True).wait_recv()
+                copy(n, w + 1, False).start()
+
+            when(ways[w][2], forward)
+        for w in (4, 1, 3):
+            when(ways[w][2], lambda w=w: copy(n, w, True).wait_recv())
 
     def finish(n):
         for w, (_, _, cond) in enumerate(ways):
@@ -224,7 +241,7 @@
     def own_apply(vec, acc):
         return block_apply(slots, lambda j: vec[j * PROBES : (j + 1) * PROBES], acc)
 
-    def gathered(k, acc):
+    def gathered(k, acc, far):
         for h in range(2):
             acc = block_apply(
                 2 * k + h,
@@ -239,9 +256,7 @@
     zero = tuple(jnp.zeros((PROBES, atoms), f32) for _ in range(ORBITALS))
     receive(0)
 
-    def bond_step(k, carry):
-        acc, total = carry
-        far[...] = jnp.dot(first[...], onehot[k], preferred_element_type=f32)
+    def bond_make(k, far):
         length = pair_row(len_ref, k)
         basis = jnp.exp(-basis_sharpness * (length - centers) ** 2)
         b_hi = basis.astype(bf16)
@@ -254,10 +269,16 @@
         blocks[2 * k, 0:PAIRS, :] = made[:, 0:atoms]
         blocks[2 * k + 1, 0:PAIRS, :] = made[:, atoms:two]
         tall[0:PAIRS, :] += jnp.abs(made[:, 0:atoms]) + jnp.abs(made[:, atoms:two])
-        return gathered(k, acc), total
+
+    def bond_step(m, acc):
+        far[...] = jnp.dot(first[...], onehot[2 * m], preferred_element_type=f32)
+        near[...] = jnp.dot(first[...], onehot[2 * m + 1], preferred_element_type=f32)
+        bond_make(2 * m, far)
+        bond_make(2 * m + 1, near)
+        return gathered(2 * m + 1, gathered(2 * m, acc, far), near)
 
     tall[0:PAIRS, :] = jnp.abs(blocks[slots, 0:PAIRS, :])
-    acc, _ = lax.fori_loop(0, slots // 2, bond_step, (own_apply(keep[0], zero), 0))
+    acc = lax.fori_loop(0, slots // 4, bond_step, own_apply(keep[0], zero))
     y1 = jnp.concatenate(acc, axis=0)
     vecs[0, :, own] = y1.astype(bf16)
     send(1)
@@ -287,16 +308,21 @@
 
     radius_copy(0).start()
 
+    def gather(n, k, buf):
+        buf[pl.ds(channels, VEC), :] = jnp.dot(vecs[n - 1], onehot[k], preferred_element_type=f32)
+
     def apply_part(n, lo, hi, acc):
-        def step(k, acc):
-            far[pl.ds(channels, VEC), :] = jnp.dot(
-                vecs[n - 1], onehot[k], preferred_element_type=f32
-            )
-            return gathered(k, acc)
-
+        def step(m, acc):
+            gather(n, 2 * m + 1, near)
+            acc = gathered(2 * m, acc, far)
+            gather(n, jnp.minimum(2 * m + 2, slots // 2 - 1), far)
+            return gathered(2 * m + 1, acc, near)
+
+        if lo == 0:
+            gather(n, 0, far)
         return lax.fori_loop(lo, hi, step, acc)
 
-    half = slots // 2
+    half = slots // 4
     acc = own_apply(y1, zero)
     radius_turn(0)
     radius_turn(1)
@@ -368,6 +394,7 @@
             pltpu.VMEM((tall_rows, atoms), f32),
             pltpu.VMEM((2 * rounds + 1, 8, atoms), f32),
             pltpu.VMEM((channels + VEC, lanes), f32),
+            pltpu.VMEM((channels + VEC, lanes), f32),
             pltpu.SemaphoreType.DMA((STEPS, 5)),
             pltpu.SemaphoreType.DMA((STEPS, 5)),
             pltpu.SemaphoreType.DMA((rounds,)),

time: 68.8 us -> 59 us (0.86)
  Pallas kernels: 65.1 us -> 54.7 us
    pallas_call x1, Pallas kernels: 65.1 us -> 54.7 us  [body(): pl.pallas_call(functools.partial(kernel, n_rows, rounds), out_shape=jax.S...]
where the time goes in v1:
time: 59 us; the launch traced here: 58.2 us
  Pallas kernels  54.7 us (93%)
  local copies, waits for them, and re-layouts  3.36 us (6%)
    pallas_call x1, Pallas kernels, body(): pl.pallas_call(functools.partial(kernel, n_rows, rounds), out_shape=jax.S...  54.7 us
    unnamed x29, local copies, waits for them, and re-layouts  2.62 us

profile of v1, /device:TPU:7, one launch (start us, length us, event | category | flops | bytes accessed | tf_op | source)
XLA Modules:
  0.0 58.2 jit_solution(10208757057160784721)
XLA Ops:
  0.0 0.0 copy-start.12
  0.0 0.9 %copy.16.wout_ref = bf16[128,169]{1,0:T(8,128)(2,1)S(1)} copy(bf16[128,169]{0,1:T(8,128)(2,1)} %param.21) | data formatting | bytes 86528 | tf_op args[7]
  0.9 0.0 copy-done.12
  0.9 0.0 copy-start.11
  1.0 0.0 copy-start.4
  1.0 0.0 copy-start.5
  1.0 0.0 copy-start.6
  1.0 0.0 copy-start.10
  1.0 0.1 copy.17.wself_ref
  1.1 0.7 %copy-done.11 = f32[1,1,128,208]{2,3,1,0:T(8,128)S(1)} copy-done((f32[1,1,128,208]{2,3,1,0:T(8,128)S(1)}, f32[1,1,128,208]{2,3,1,0:T(8,128)}, u32[]{:S(2)}) %copy-start.11) | copy-done | bytes 106520
  1.8 0.0 copy-start
  1.8 0.0 copy-start.1
  1.8 0.0 copy-start.2
  1.8 0.0 copy-start.3
  1.8 0.0 copy-start.7
  1.9 0.1 copy.15
  2.0 0.0 copy-start.8
  2.0 0.0 copy-start.9
  2.0 0.0 copy-done.4
  2.0 0.0 copy-done.5
  2.0 0.0 copy-done.6
  2.0 0.0 copy-done.10
  2.0 0.6 %copy-done = bf16[1,1,128,256]{3,2,1,0:T(8,128)(2,1)S(1)} copy-done((bf16[1,1,128,256]{3,2,1,0:T(8,128)(2,1)S(1)}, bf16[1,1,128,256]{3,2,1,0:T(8,128)(2,1)}, u32[]{:S(2)}) %copy-start) | copy-done | bytes 65560
  2.7 0.0 copy-done.1
  2.7 0.0 copy-done.2
  2.7 0.0 copy-done.3
  2.7 0.0 copy-done.7
  2.7 0.0 copy-done.8
  2.7 0.0 copy-done.9
  2.8 54.7 %shard_map.136 = f32[128,208]{1,0:T(8,128)S(1)} custom-call(bf16[128,256]{1,0:T(8,128)(2,1)S(1)} %bitcast.9, s32[1,128]{1,0:T(1,128)S(1)} %bitcast.13, bf16[2,256]{1,0:T(2,128)(2,1)S(1)} %copy-done.8, bf16[256,128]{1,0:T(8,128)(2,1)S(1)} %copy-done.1, bf16[256,128]{1,0:T(8,128)(2,1)S(1)} %copy-done.2, f32[16,128]{1,0:T(8,128)S(1)} %copy-done.7, ...), custom_call_target="tpu_custom_call" | custom-call | tf_op jit(solution)/shard_map/pallas_call | solution.py:379
  57.5 0.7 %copy.18 = f32[1,1,128,208]{2,3,1,0:T(8,128)} copy(f32[1,1,128,208]{3,2,1,0:T(8,128)S(1)} %bitcast.7) | data formatting | bytes 212992 | tf_op jit(solution)/shard_map/broadcast_in_dim | solution.py:410
Async XLA Ops:
  0.0 0.9 %copy-start.12 = (bf16[256,169]{0,1:T(8,128)(2,1)S(1)}, bf16[256,169]{0,1:T(8,128)(2,1)}, u32[]{:S(2)}) copy-start(bf16[256,169]{0,1:T(8,128)(2,1)} %param.22) | copy-start | bytes 259588
  0.9 0.9 %copy-start.11 = (f32[1,1,128,208]{2,3,1,0:T(8,128)S(1)}, f32[1,1,128,208]{2,3,1,0:T(8,128)}, u32[]{:S(2)}) copy-start(f32[1,1,128,208]{2,3,1,0:T(8,128)} %param.26) | copy-start | bytes 319492
  1.0 1.0 %copy-start.4 = (s32[1,1,24,128]{3,2,1,0:T(8,128)S(1)}, s32[1,1,24,128]{3,2,1,0:T(8,128)}, u32[]{:S(2)}) copy-start(s32[1,1,24,128]{3,2,1,0:T(8,128)} %param.23) | copy-start | bytes 36868
  1.0 1.0 %copy-start.5 = (s32[1,1,24,128]{3,2,1,0:T(8,128)S(1)}, s32[1,1,24,128]{3,2,1,0:T(8,128)}, u32[]{:S(2)}) copy-start(s32[1,1,24,128]{3,2,1,0:T(8,128)} %param.24) | copy-start | bytes 36868
  1.0 1.0 %copy-start.6 = (f32[1,1,24,128]{3,2,1,0:T(8,128)S(1)}, f32[1,1,24,128]{3,2,1,0:T(8,128)}, u32[]{:S(2)}) copy-start(f32[1,1,24,128]{3,2,1,0:T(8,128)} %param.25) | copy-start | bytes 36868
  1.0 1.0 %copy-start.10 = (f32[5]{0:T(128)S(1)}, f32[5]{0:T(128)}, u32[]{:S(2)}) copy-start(f32[5]{0:T(128)} %coef_ref.1) | copy-start | bytes 64
  1.8 0.8 %copy-start = (bf16[1,1,128,256]{3,2,1,0:T(8,128)(2,1)S(1)}, bf16[1,1,128,256]{3,2,1,0:T(8,128)(2,1)}, u32[]{:S(2)}) copy-start(bf16[1,1,128,256]{3,2,1,0:T(8,128)(2,1)} %param.14) | copy-start | bytes 196612
  1.8 0.9 %copy-start.1 = (bf16[256,128]{1,0:T(8,128)(2,1)S(1)}, bf16[256,128]{1,0:T(8,128)(2,1)}, u32[]{:S(2)}) copy-start(bf16[256,128]{1,0:T(8,128)(2,1)} %wsrc_ref.1) | copy-start | bytes 196612
  1.8 0.9 %copy-start.2 = (bf16[256,128]{1,0:T(8,128)(2,1)S(1)}, bf16[256,128]{1,0:T(8,128)(2,1)}, u32[]{:S(2)}) copy-start(bf16[256,128]{1,0:T(8,128)(2,1)} %wdst_ref.1) | copy-start | bytes 196612
  1.8 0.9 %copy-start.3 = (bf16[128,128]{1,0:T(8,128)(2,1)S(1)}, bf16[128,128]{1,0:T(8,128)(2,1)}, u32[]{:S(2)}) copy-start(bf16[128,128]{1,0:T(8,128)(2,1)} %wmid_ref.1) | copy-start | bytes 98308
  1.8 0.9 %copy-start.7 = (f32[16,128]{1,0:T(8,128)S(1)}, f32[16,128]{1,0:T(8,128)}, u32[]{:S(2)}) copy-start(f32[16,128]{1,0:T(8,128)} %wrad_ref.1) | copy-start | bytes 24580
  2.0 0.8 %copy-start.8 = (bf16[2,256]{1,0:T(2,128)(2,1)S(1)}, bf16[2,256]{1,0:T(2,128)(2,1)}, u32[]{:S(2)}) copy-start(bf16[2,256]{1,0:T(2,128)(2,1)} %embed_ref.1) | copy-start | bytes 3076
  2.0 0.8 %copy-start.9 = (s32[1,1,128]{2,1,0:T(1,128)S(1)}, s32[1,1,128]{2,1,0:T(1,128)}, u32[]{:S(2)}) copy-start(s32[1,1,128]{2,1,0:T(1,128)} %param.15) | copy-start | bytes 1540
